TPU v7x, 512 devices: a whole 4x8x8 slice. The times are simulated.
512 devices in a mesh: dp: 32 (over z, x), tensor: 16 (over y, core).
Axes of the slice: x: 4, y: 8, z: 8, core: 2. Of those that a mesh axis runs over, the one named last changes fastest.
Arguments:
- grads_out: bfloat16 [1024, 28672], P('dp'), may hold values from -6 to 6
- inputs: bfloat16 [1024, 8192], P('dp'), may hold values from -6 to 6
- basis_out: bfloat16 [28672, 14336], P('dp', 'tensor'), may hold values from -0.03125 to 0.03125
- basis_in: bfloat16 [8192, 4096], P('tensor', 'dp'), may hold values from -0.0625 to 0.0625
- lengths: int32 [32], P('dp'), may hold values from 1 to 32, as said below
Outputs:
- corrections: float32 [14336, 4096], P('tensor', 'dp')
Inputs may be any that keep to these rules, and one draw needn't show every extreme that they name: `lengths`: every sequence has at least one live token, and some sequence has all 32 slots live.
All inputs are finite; a program needn't handle non-finite values.
Results may differ from a plain program's by a relative error of at most 0.0026.
Values may be sent and summed in bfloat16 or wider, within the bound.
No kernel may reach another device: no remote copies, remote signals or barrier semaphores. Data moves between devices by JAX's collectives and lax.ppermute only.
A program may use at most 64 MiB of HBM per device.

v0:
```python
import jax
import jax.numpy as jnp
from jax import lax
from jax.sharding import PartitionSpec as P


def per_device(grads_out, inputs, basis_out, basis_in, lengths):
    seq_len = grads_out.shape[0]
    positions = jnp.arange(seq_len)
    live = positions[:, None] < lengths[0]
    masked = jnp.where(live, grads_out, jnp.zeros_like(grads_out))
    gathered = lax.all_to_all(masked, "dp", split_axis=1, concat_axis=0, tiled=True)
    partial_sum = jnp.dot(gathered, basis_out, preferred_element_type=jnp.float32)
    rotated = lax.psum(partial_sum, "dp").astype(jnp.bfloat16)
    width_in = inputs.shape[1] // lax.axis_size("tensor")
    column_slab = lax.dynamic_slice_in_dim(inputs, lax.axis_index("tensor") * width_in, width_in, 1)
    partial_in = jnp.dot(
        lax.all_gather(column_slab, "dp", axis=0, tiled=True),
        basis_in,
        preferred_element_type=jnp.float32,
    )
    panel = lax.psum(partial_in, "tensor").astype(jnp.bfloat16)
    row_total = rotated.shape[0]
    sequences = row_total // seq_len
    group_size = 4
    number_of_blocks = sequences // group_size
    rotated_blocks = rotated.reshape(number_of_blocks, group_size, seq_len, rotated.shape[1])
    panel_block_list = panel.reshape(number_of_blocks, group_size, seq_len, panel.shape[1])

    def accumulate(total, pair):
        left_factor, right_factor = pair
        sample_case = jnp.einsum(
            "qjt,qjr->qtr", left_factor, right_factor, preferred_element_type=jnp.float32
        )
        return (total + jnp.sum(sample_case * sample_case, axis=0), None)

    initial_total = jnp.zeros((rotated.shape[1], panel.shape[1]), jnp.float32)
    total, unused = lax.scan(accumulate, initial_total, (rotated_blocks, panel_block_list))
    return total / row_total


def solution(mesh):
    placed = (P("dp", None), P("dp", None), P("dp", "tensor"), P("tensor", "dp"), P("dp"))
    return jax.shard_map(
        per_device, mesh=mesh, in_specs=placed, out_specs=P("tensor", "dp"), check_vma=False
    )
```

profile of v0, /device:TPU:24, one launch (start us, length us, event | category | flops | bytes accessed | tf_op | source)
XLA Modules:
  0.0 366.4 jit_solution(3044291850052730541)
XLA Ops:
  7.3 1.7 broadcast_select_fusion
  9.0 1.4 copy.10
  10.4 13.4 %all-to-all-start = ((bf16[32,32,896]{2,0,1:T(8,128)(2,1)}), bf16[32,32,896]{2,0,1:T(8,128)(2,1)}, u32[]{:S(2)}, u32[]{:S(2)}) async-start(bf16[32,32,896]{2,0,1:T(8,128)(2,1)} %bitcast.19), calls=%async_computation | async-start | bytes 3670016 | tf_op jit(solution)/shard_map/all_to_all | solution.py:12
  23.9 1.4 constant_dynamic-slice_fusion
  25.3 88.1 %all-gather.2.cloned.1.call-done = bf16[1024,512]{1,0:T(8,128)(2,1)} async-done(((bf16[32,512]{1,0:T(8,128)(2,1)}), bf16[1024,512]{1,0:T(8,128)(2,1)}) %all-gather.2.cloned.1.call-update) | async-done | bytes 1048592 | tf_op jit(solution)/shard_map/all_gather | solution.py:18
  113.4 1.7 fusion.6
  115.1 50.1 %all-reduce.3 = bf16[1024,128]{1,0:T(8,128)(2,1)S(1)} all-reduce(f32[1024,128]{1,0:T(8,128)S(1)} %fusion.6), channel_id=1, replica_groups=mesh['dp'=32,'tensor'=16] {'tensor'}, use_global_device_ids=true, to_apply=%region_1.2 | all-reduce | flops 131072 | bytes 786432 | tf_op jit(solution)/shard_map/psum | solution.py:22
  165.2 5.5 %fusion.5 = f32[1024,896]{1,0:T(8,128)} fusion(bf16[1024,896]{1,0:T(8,128)(2,1)} %bitcast.2, bf16[896,896]{1,0:T(8,128)(2,1)S(1)} %copy-done), kind=kOutput, calls=%fused_computation.12 | convolution fusion | flops 1644167168 | bytes 7110656 | tf_op jit(solution)/shard_map/dot_general | solution.py:13
  170.8 175.2 %all-reduce.2 = bf16[1024,896]{1,0:T(8,128)(2,1)} all-reduce(f32[1024,896]{1,0:T(8,128)} %fusion.5), channel_id=1, replica_groups=mesh['dp'=32,'tensor'=16] {'dp'}, use_global_device_ids=true, to_apply=%region_0.1 | all-reduce | flops 917504 | bytes 5505024 | tf_op jit(solution)/shard_map/psum | solution.py:14
  346.0 12.8 %while.11 = (s32[]{:T(128)}, f32[896,128]{1,0:T(8,128)S(1)}, bf16[8,4,32,896]{3,2,1,0:T(8,128)(2,1)}, bf16[8,4,32,128]{3,2,1,0:T(8,128)(2,1)S(1)}, s32[]{:T(128)}, /*index=5*/s32[]{:T(128)}) while((s32[]{:T(128)}, f32[896,128]{1,0:T(8,128)S(1)}, bf16[8,4,32,896]{3,2,1,0:T(8,128)(2,1)}, bf16[8,4,32,128]{3,2,1,0:T(8,128)(2,1)S(1)}, ...), condition=%wide.region_4.5_spmd.clone, body=%wide.region_2.4_spmd.clone.sunk | while | flops 30392320 | bytes 2098263 | solution.py:38
  346.0 1.4 multiply_reduce_fusion.2
  347.4 0.1 select_add_fusion.2
  347.6 1.4 multiply_reduce_fusion.2
  349.0 0.1 select_add_fusion.2
  349.2 1.4 multiply_reduce_fusion.2
  350.6 0.1 select_add_fusion.2
  350.8 1.4 multiply_reduce_fusion.2
  352.2 0.1 select_add_fusion.2
  352.4 1.4 multiply_reduce_fusion.2
  353.8 0.1 select_add_fusion.2
  354.0 1.4 multiply_reduce_fusion.2
  355.6 1.4 multiply_reduce_fusion.2
  357.2 1.4 multiply_reduce_fusion.2
  358.7 0.8 broadcast_multiply_fusion
  (12 shorter events, 0.4 us)
Async XLA Ops:
  6.5 158.7 %copy-start = (bf16[896,896]{1,0:T(8,128)(2,1)S(1)}, bf16[896,896]{1,0:T(8,128)(2,1)}, u32[]{:S(2)}) copy-start(bf16[896,896]{1,0:T(8,128)(2,1)} %param.9) | copy-start | bytes 4816900
  10.4 103.0 %copy-start.1 = (bf16[512,128]{1,0:T(8,128)(2,1)S(1)}, bf16[512,128]{1,0:T(8,128)(2,1)}, u32[]{:S(2)}) copy-start(bf16[512,128]{1,0:T(8,128)(2,1)} %param.10) | copy-start | bytes 393220
  10.4 154.8 %all-to-all-start = ((bf16[32,32,896]{2,0,1:T(8,128)(2,1)}), bf16[32,32,896]{2,0,1:T(8,128)(2,1)}, u32[]{:S(2)}, u32[]{:S(2)}) async-start(bf16[32,32,896]{2,0,1:T(8,128)(2,1)} %bitcast.19), calls=%async_computation | async-start | bytes 3670016 | tf_op jit(solution)/shard_map/all_to_all | solution.py:12
  23.8 89.6 %all-gather.2.cloned.1.call-start = ((), (), s32[]{:S(2)}) async-start(), calls=%async_computation.1 | async-start | bytes 1081344 | tf_op jit(solution)/shard_map/all_gather | solution.py:18
Sparse Core Ops, SparseCore 0:
  27.9 85.5 all-gather.1
where the time goes:
time: 367 us; the launch traced here: 366 us
  blocking collectives  225 us (61%)
  waiting for transfers between devices  88.1 us (24%)
  matrix products  18.8 us (5%)
  between operations  14.2 us (4%)
  starting transfers between devices  13.5 us (4%)
    psum x1, blocking collectives, per_device(): rotated = lax.psum(partial_sum, 'dp').astype(jnp.bfloat16)  175 us
    all_gather x1, waiting for transfers between devices, per_device(): lax.all_gather(column_slab, 'dp', axis=0, tiled=True)  88.1 us
    psum x1, blocking collectives, per_device(): panel = lax.psum(partial_in, 'tensor').astype(jnp.bfloat16)  50.1 us
    all_to_all x1, starting transfers between devices, per_device(): lax.all_to_all(masked, 'dp', split_axis=1, concat_axis=0, tiled=True)  13.4 us
    dot_general x8, matrix products, accumulate(): jnp.einsum('qjt,qjr->qtr', left_factor, right_factor, preferred_element_t...  11.6 us
  transfers between devices with their start and end apart: 2, of which 1 were waited for; matrix products, arithmetic and copies ran while one was open for 1% of the time, Pallas kernels for 0%

commit v1 on v0

--- a/solution.py
+++ b/solution.py
@@ -15,7 +15,9 @@
     width_in = inputs.shape[1] // lax.axis_size("tensor")
     column_slab = lax.dynamic_slice_in_dim(inputs, lax.axis_index("tensor") * width_in, width_in, 1)
     partial_in = jnp.dot(
-        lax.all_gather(column_slab, "dp", axis=0, tiled=True),
+        jnp.concatenate(
+            lax.all_to_all(jnp.stack([column_slab] * lax.axis_size("dp")), "dp", 0, 0), axis=0
+        ),
         basis_in,
         preferred_element_type=jnp.float32,
     )

time: 367 us -> 300 us (0.82)
  waiting for transfers between devices: 88.1 us -> 24.3 us
  between operations: 14.2 us -> 0.73 us
  starting transfers between devices: 13.5 us -> 19 us
  blocking collectives: 225 us -> 230 us
    all_gather x1 -> x0, waiting for transfers between devices: 88.1 us -> none  [per_device(): lax.all_gather(column_slab, 'dp', axis=0, tiled=True)]
    all_to_all x0 -> x1, waiting for transfers between devices: none -> 24.3 us  [per_device(): lax.all_to_all(jnp.stack([column_slab] * lax.axis_size('dp')), 'dp', 0, 0)]
    all_to_all x0 -> x1, starting transfers between devices: none -> 13.2 us  [per_device(): lax.all_to_all(jnp.stack([column_slab] * lax.axis_size('dp')), 'dp', 0, 0)]
    all_to_all x1, starting transfers between devices: 13.4 us -> 5.79 us  [per_device(): lax.all_to_all(masked, 'dp', split_axis=1, concat_axis=0, tiled=True)]
where the time goes in v1:
time: 300 us
  blocking collectives  230 us (77%)
  waiting for transfers between devices  24.3 us (8%)
  starting transfers between devices  19 us (6%)
  matrix products  18.4 us (6%)
  other arithmetic  3.45 us (1%)
  local copies, waits for them, and re-layouts  3.41 us (1%)
    psum x1, blocking collectives, per_device(): rotated = lax.psum(partial_sum, 'dp').astype(jnp.bfloat16)  177 us
    psum x1, blocking collectives, per_device(): panel = lax.psum(partial_in, 'tensor').astype(jnp.bfloat16)  53 us
    all_to_all x1, waiting for transfers between devices, per_device(): lax.all_to_all(jnp.stack([column_slab] * lax.axis_size('dp')), 'dp', 0, 0)  24.3 us
    all_to_all x1, starting transfers between devices, per_device(): lax.all_to_all(jnp.stack([column_slab] * lax.axis_size('dp')), 'dp', 0, 0)  13.2 us
    dot_general x8, matrix products, accumulate(): jnp.einsum('qjt,qjr->qtr', left_factor, right_factor, preferred_element_t...  11.6 us
  transfers between devices with their start and end apart: 2, of which 1 were waited for; matrix products, arithmetic and copies ran while one was open for 1% of the time, Pallas kernels for 0%

profile of v1, /device:TPU:24, one launch (start us, length us, event | category | flops | bytes accessed | tf_op | source)
XLA Modules:
  0.0 299.6 jit_solution(2615055594585570711)
XLA Ops:
  0.0 0.9 constant_dynamic-slice_fusion
  0.9 1.1 stack.2
  2.0 13.2 %all-to-all-start.1 = ((bf16[32,32,512]{2,1,0:T(8,128)(2,1)}), bf16[32,32,512]{2,1,0:T(8,128)(2,1)S(1)}, u32[]{:S(2)}, u32[]{:S(2)}) async-start(bf16[32,32,512]{2,1,0:T(8,128)(2,1)} %stack.2), calls=%async_computation.1 | async-start | bytes 2097152 | tf_op jit(solution)/shard_map/all_to_all | solution.py:19
  15.8 1.7 broadcast_select_fusion
  17.5 1.4 copy.10
  18.9 24.3 %all-to-all-done.1 = bf16[32,32,512]{2,1,0:T(8,128)(2,1)S(1)} async-done(((bf16[32,32,512]{2,1,0:T(8,128)(2,1)}), bf16[32,32,512]{2,1,0:T(8,128)(2,1)S(1)}, u32[]{:S(2)}, u32[]{:S(2)}) %all-to-all-start.1) | async-done | bytes 1048608 | tf_op jit(solution)/shard_map/all_to_all | solution.py:19
  43.3 5.8 %all-to-all-start = ((bf16[32,32,896]{2,0,1:T(8,128)(2,1)}), bf16[32,32,896]{2,0,1:T(8,128)(2,1)}, u32[]{:S(2)}, u32[]{:S(2)}) async-start(bf16[32,32,896]{2,0,1:T(8,128)(2,1)} %bitcast.20), calls=%async_computation | async-start | bytes 3670016 | tf_op jit(solution)/shard_map/all_to_all | solution.py:12
  49.1 1.2 fusion.6
  50.3 53.0 %all-reduce.3 = bf16[1024,128]{1,0:T(8,128)(2,1)S(1)} all-reduce(f32[1024,128]{1,0:T(8,128)} %fusion.6), channel_id=1, replica_groups=mesh['dp'=32,'tensor'=16] {'tensor'}, use_global_device_ids=true, to_apply=%region_1.2 | all-reduce | flops 131072 | bytes 786432 | tf_op jit(solution)/shard_map/psum | solution.py:24
  103.4 5.5 %fusion.5 = f32[1024,896]{1,0:T(8,128)} fusion(bf16[1024,896]{1,0:T(8,128)(2,1)} %bitcast.2, bf16[896,896]{1,0:T(8,128)(2,1)S(1)} %copy-done), kind=kOutput, calls=%fused_computation.12 | convolution fusion | flops 1644167168 | bytes 7110656 | tf_op jit(solution)/shard_map/dot_general | solution.py:13
  108.9 177.0 %all-reduce.2 = bf16[1024,896]{1,0:T(8,128)(2,1)} all-reduce(f32[1024,896]{1,0:T(8,128)} %fusion.5), channel_id=1, replica_groups=mesh['dp'=32,'tensor'=16] {'dp'}, use_global_device_ids=true, to_apply=%region_0.1 | all-reduce | flops 917504 | bytes 5505024 | tf_op jit(solution)/shard_map/psum | solution.py:14
  286.0 12.8 %while.11 = (s32[]{:T(128)}, f32[896,128]{1,0:T(8,128)S(1)}, bf16[8,4,32,896]{3,2,1,0:T(8,128)(2,1)}, bf16[8,4,32,128]{3,2,1,0:T(8,128)(2,1)S(1)}, s32[]{:T(128)}, /*index=5*/s32[]{:T(128)}) while((s32[]{:T(128)}, f32[896,128]{1,0:T(8,128)S(1)}, bf16[8,4,32,896]{3,2,1,0:T(8,128)(2,1)}, bf16[8,4,32,128]{3,2,1,0:T(8,128)(2,1)S(1)}, ...), condition=%wide.region_4.5_spmd.clone, body=%wide.region_2.4_spmd.clone.sunk | while | flops 30392320 | bytes 2098263 | solution.py:40
  286.0 1.4 multiply_reduce_fusion.2
  287.4 0.1 select_add_fusion.2
  287.6 1.4 multiply_reduce_fusion.2
  289.0 0.1 select_add_fusion.2
  289.2 1.4 multiply_reduce_fusion.2
  290.6 0.1 select_add_fusion.2
  290.8 1.4 multiply_reduce_fusion.2
  292.4 1.4 multiply_reduce_fusion.2
  294.0 1.4 multiply_reduce_fusion.2
  295.6 1.4 multiply_reduce_fusion.2
  297.2 1.4 multiply_reduce_fusion.2
  298.8 0.8 broadcast_multiply_fusion
  (12 shorter events, 0.6 us)
Async XLA Ops:
  0.0 103.4 %copy-start = (bf16[896,896]{1,0:T(8,128)(2,1)S(1)}, bf16[896,896]{1,0:T(8,128)(2,1)}, u32[]{:S(2)}) copy-start(bf16[896,896]{1,0:T(8,128)(2,1)} %param.9) | copy-start | bytes 4816900
  2.0 41.3 %all-to-all-start.1 = ((bf16[32,32,512]{2,1,0:T(8,128)(2,1)}), bf16[32,32,512]{2,1,0:T(8,128)(2,1)S(1)}, u32[]{:S(2)}, u32[]{:S(2)}) async-start(bf16[32,32,512]{2,1,0:T(8,128)(2,1)} %stack.2), calls=%async_computation.1 | async-start | bytes 2097152 | tf_op jit(solution)/shard_map/all_to_all | solution.py:19
  43.3 5.8 %copy-start.1 = (bf16[512,128]{1,0:T(8,128)(2,1)S(1)}, bf16[512,128]{1,0:T(8,128)(2,1)}, u32[]{:S(2)}) copy-start(bf16[512,128]{1,0:T(8,128)(2,1)} %param.10) | copy-start | bytes 393220
  43.3 60.1 %all-to-all-start = ((bf16[32,32,896]{2,0,1:T(8,128)(2,1)}), bf16[32,32,896]{2,0,1:T(8,128)(2,1)}, u32[]{:S(2)}, u32[]{:S(2)}) async-start(bf16[32,32,896]{2,0,1:T(8,128)(2,1)} %bitcast.20), calls=%async_computation | async-start | bytes 3670016 | tf_op jit(solution)/shard_map/all_to_all | solution.py:12
